TPU v7x, 32 devices: a whole 2x2x4 slice. The times are simulated.
32 devices in a mesh: row: 4 (over y, x), col: 8 (over z, core).
Axes of the slice: x: 2, y: 2, z: 4, core: 2. Of those that a mesh axis runs over, the one named last changes fastest.
Arguments:
- points: float32 [8, 32768], P(None, ('row', 'col')), may hold values from -4 to 4
- point_order: int32 [32, 1024], P(('row', 'col')), may hold values from 0 to 1023, each once within a row
- noise_var: float32 [32768], P(('row', 'col')), may hold values from 0.1 to 3
- inv_scale: float32 [8], replicated, may hold values from 0.2 to 0.6
- basis_vectors: float32 [16, 64, 32768], P(None, None, ('row', 'col')), may hold values from -4 to 4
- current: float32 [64, 32768], P(None, ('row', 'col')), may hold values from -22 to 22
- tile_rows: int32 [4, 8, 64], P('row', 'col'), may hold values from 0 to 31, as said below
- tile_cols: int32 [4, 8, 64], P('row', 'col'), may hold values from 0 to 15
Outputs:
- lanczos_next: float32 [64, 32768], P(None, ('row', 'col'))
- coefficients: float32 [4, 64], replicated
- gradient_product: float32 [64, 32768], P(None, ('row', 'col'))
Inputs may be any that keep to these rules, and one draw needn't show every extreme that they name: In each grid cell the 64 pairs (tile_rows, tile_cols) are distinct; each cell lists its 4 pairs with I = J; over all cells no unordered pair of distinct blocks is listed twice: it is listed as (I, J) with I < J when I + J is odd and with I > J when I + J is even.
All inputs are finite; a program needn't handle non-finite values.
Results may differ from a plain program's by a relative error of at most 0.00019.
Values sent between devices are 32-bit elements; how exact they have to be, the bound alone decides.
A program may use at most 128 MiB of HBM per device.

v0:
```python
import math

import jax
import jax.numpy as jnp
from jax import lax
from jax.sharding import PartitionSpec as P

BLOCK = 256
ITERS = 2


ROOT_THREE = math.sqrt(3.0)
SUPPORT = 3.0
EPSILON = 1e-06
HIGHEST = lax.Precision.HIGHEST


def kernel_tiles(row_points, col_points):
    dist_sq = jnp.zeros(
        (row_points.shape[1], row_points.shape[2], col_points.shape[2]), jnp.float32
    )
    for feature in range(row_points.shape[0]):
        differ = row_points[feature][:, :, None] - col_points[feature][:, None, :]
        dist_sq = dist_sq + differ * differ
    shifted = dist_sq + EPSILON
    radius = jnp.sqrt(shifted)
    decaying = jnp.exp(-ROOT_THREE * radius)
    matern_part = (1.0 + ROOT_THREE * radius) * decaying
    tapered = jnp.maximum(1.0 - radius / SUPPORT, 0.0)
    taper_cube = tapered * tapered * tapered
    weight = taper_cube * tapered * (1.0 + 4.0 * radius / SUPPORT)
    kernel_tile = matern_part * weight
    slope_tile = shifted * (
        3.0 * decaying * weight + 20.0 * matern_part * taper_cube / (SUPPORT * SUPPORT)
    )
    return (kernel_tile, slope_tile)


def tile_products(
    col_values, row_values, col_points, row_points, row_blocks, col_blocks, mirror_mask, with_slope
):
    probe_count = col_values.shape[0]
    block_len = col_values.shape[2]
    group_size = math.gcd(row_blocks.shape[0], 8)
    layers = 2 if with_slope else 1
    row_total = jnp.zeros((layers, probe_count, row_values.shape[1], block_len), jnp.float32)
    col_total = jnp.zeros((layers, probe_count, col_values.shape[1], block_len), jnp.float32)
    grouped = (
        row_blocks.reshape(-1, group_size),
        col_blocks.reshape(-1, group_size),
        mirror_mask.reshape(-1, group_size),
    )

    def one_group(carried, listed):
        row_acc, col_acc = carried
        row_pick, col_pick, mirror_pick = listed
        kernel_tile, slope_tile = kernel_tiles(
            jnp.take(row_points, row_pick, axis=1), jnp.take(col_points, col_pick, axis=1)
        )
        if with_slope:
            stacked = jnp.stack([kernel_tile, slope_tile])
        else:
            stacked = kernel_tile[None]
        col_side = jnp.take(col_values, col_pick, axis=1)
        row_side = jnp.take(row_values, row_pick, axis=1) * mirror_pick[None, :, None]
        direct = jnp.einsum("pgj,kgij->kpgi", col_side, stacked, precision=HIGHEST)
        mirrored = jnp.einsum("pgi,kgij->kpgj", row_side, stacked, precision=HIGHEST)
        return (
            (row_acc.at[:, :, row_pick].add(direct), col_acc.at[:, :, col_pick].add(mirrored)),
            None,
        )

    (row_total, col_total), unused = lax.scan(one_group, (row_total, col_total), grouped)
    return (
        row_total.reshape(layers * probe_count, -1),
        col_total.reshape(layers * probe_count, -1),
    )


def both_sides(stacked):
    col_side = lax.all_gather(stacked, "row", axis=1, tiled=True)
    row_side = lax.all_gather(stacked, "col", axis=1, tiled=True)
    return (col_side, row_side)


def reduce_parts(row_part, col_part):
    from_rows = lax.psum_scatter(row_part, "col", scatter_dimension=1, tiled=True)
    from_cols = lax.psum_scatter(col_part, "row", scatter_dimension=1, tiled=True)
    return from_rows + from_cols


def on_device(
    points, point_order, noise_var, inv_scale, basis_vectors, current, tile_rows, tile_cols
):
    feature_count = points.shape[0]
    probe_count = current.shape[0]
    per_device = points.shape[1]
    block_count = per_device // BLOCK
    row_count = lax.axis_size("row")
    col_count = lax.axis_size("col")
    point_total = per_device * row_count * col_count
    arrangement = point_order[0]
    scaled = jnp.take(points, arrangement, axis=1) * inv_scale[:, None]
    noise_here = jnp.take(noise_var, arrangement)
    row_blocks = tile_rows[0, 0]
    col_blocks = tile_cols[0, 0]
    global_row = lax.axis_index("row") * col_count * block_count + row_blocks
    global_col = (
        col_blocks // block_count * col_count + lax.axis_index("col")
    ) * block_count + col_blocks % block_count
    mirror_mask = (global_row != global_col).astype(jnp.float32)
    earlier = basis_vectors
    coefficient_rows = []
    gradient_product = current
    col_points = scaled
    row_points = scaled
    for iteration in range(ITERS):
        if iteration == 0:
            stacked = jnp.concatenate([scaled, current], axis=0)
            apply_col_side, apply_row_side = both_sides(stacked)
            apply_col_points = apply_col_side[:feature_count].reshape(feature_count, -1, BLOCK)
            apply_row_points = apply_row_side[:feature_count].reshape(feature_count, -1, BLOCK)
            apply_row_part, apply_col_part = tile_products(
                apply_col_side[feature_count:].reshape(probe_count, -1, BLOCK),
                apply_row_side[feature_count:].reshape(probe_count, -1, BLOCK),
                apply_col_points,
                apply_row_points,
                row_blocks,
                col_blocks,
                mirror_mask,
                True,
            )
            summed = reduce_parts(apply_row_part, apply_col_part)
            image_vec = summed[:probe_count] + noise_here * current
            gradient_product = summed[probe_count:]
            col_points = apply_col_points
            row_points = apply_row_points
        else:
            col_side, row_side = both_sides(current)
            row_part, col_part = tile_products(
                col_side.reshape(probe_count, -1, BLOCK),
                row_side.reshape(probe_count, -1, BLOCK),
                col_points,
                row_points,
                row_blocks,
                col_blocks,
                mirror_mask,
                False,
            )
            image_vec = reduce_parts(row_part, col_part) + noise_here * current
        earlier_dots, alpha_now = lax.psum(
            (
                jnp.einsum("hpn,pn->hp", earlier, image_vec, precision=HIGHEST),
                jnp.sum(current * image_vec, axis=1),
            ),
            ("row", "col"),
        )
        earlier_dots = earlier_dots / point_total
        alpha_now = alpha_now / point_total
        residual_vec = (
            image_vec
            - alpha_now[:, None] * current
            - jnp.einsum("hp,hpn->pn", earlier_dots, earlier, precision=HIGHEST)
        )
        residual_sq = (
            lax.psum(jnp.sum(residual_vec * residual_vec, axis=1), ("row", "col")) / point_total
        )
        beta_now = jnp.sqrt(residual_sq + EPSILON)
        coefficient_rows += [alpha_now, beta_now]
        if iteration + 1 < ITERS:
            earlier = jnp.concatenate([earlier, current[None]], axis=0)
        current = residual_vec / beta_now[:, None]
    return (current, jnp.stack(coefficient_rows), gradient_product)


def solution(mesh):
    return jax.shard_map(
        on_device,
        mesh=mesh,
        in_specs=(
            P(None, ("row", "col")),
            P(("row", "col"), None),
            P(("row", "col")),
            P(),
            P(None, None, ("row", "col")),
            P(None, ("row", "col")),
            P("row", "col", None),
            P("row", "col", None),
        ),
        out_specs=(P(None, ("row", "col")), P(), P(None, ("row", "col"))),
        check_vma=False,
    )
```

profile of v0, /device:TPU:0, one launch (start us, length us, event | category | flops | bytes accessed | tf_op | source)
XLA Modules:
  0.0 1059.3 jit_solution(18211700284543774022)
XLA Ops:
  17.7 27.1 %all-gather.7.cloned.1.call-done = f32[72,4096]{1,0:T(8,128)} async-done(((f32[72,1024]{1,0:T(8,128)}), f32[72,4096]{1,0:T(8,128)}) %all-gather.7.cloned.1.call-update) | async-done | bytes 1179664 | tf_op jit(solution)/shard_map/all_gather | solution.py:81
  47.2 30.9 %all-gather.5.cloned.1.call-done = f32[72,8192]{1,0:T(8,128)} async-done(((f32[72,1024]{1,0:T(8,128)}), f32[72,8192]{1,0:T(8,128)}) %all-gather.5.cloned.1.call-update) | async-done | bytes 2359312 | tf_op jit(solution)/shard_map/all_gather | solution.py:82
  85.4 256.3 %while.30 = (s32[]{:T(128)}, f32[2,64,32,256]{3,1,2,0:T(8,128)}, f32[2,64,16,256]{3,1,2,0:T(8,128)}, s32[8,8]{1,0:T(8,128)S(1)}, f32[8,32,256]{2,0,1:T(8,128)S(1...) while((s32[]{:T(128)}, f32[2,64,32,256]{3,1,2,0:T(8,128)}, ...), condition=%wide.region_3.8_spmd, body=%wide.region_0.7_spmd.sunk | while | flops 1637255296 | bytes 25309028 | solution.py:73
  363.1 19.3 %reduce-scatter.7.cloned.1.call-done = f32[128,1024]{1,0:T(8,128)} async-done(((f32[128,4096]{1,0:T(8,128)}), f32[128,1024]{1,0:T(8,128)}) %reduce-scatter.7.cloned.1.call-update) | async-done | bytes 524304 | tf_op jit(solution)/shard_map/reduce_scatter | solution.py:88
  382.4 52.3 %reduce-scatter.5.cloned.1.call-done = f32[128,1024]{1,0:T(8,128)} async-done(((f32[128,8192]{1,0:T(8,128)}), f32[128,1024]{1,0:T(8,128)}) %reduce-scatter.5.cloned.1.call-update) | async-done | bytes 524304 | tf_op jit(solution)/shard_map/reduce_scatter | solution.py:87
  436.1 9.0 fusion.67
  445.1 38.1 %all-reduce.1 = (f32[16,64]{0,1:T(8,128)S(1)}, f32[64]{0:T(128)S(1)}) all-reduce(f32[16,64]{0,1:T(8,128)S(1)} %bitcast.439, f32[64]{0:T(128)S(1)} %get-tuple-element.445), channel_id=1, replica_groups=mesh['row'=4,'col'=8] {'row','col'}, use_global_device_ids=true, to_apply=%region_8.13 | all-reduce | flops 1088 | bytes 8704 | tf_op jit(solution)/shard_map/psum | solution.py:151
  491.2 41.6 %psum.44 = f32[64]{0:T(128)S(1)} all-reduce(f32[64]{0:T(128)S(1)} %get-tuple-element.401), channel_id=1, replica_groups=mesh['row'=4,'col'=8] {'row','col'}, use_global_device_ids=true, to_apply=%region_10.15 | all-reduce | flops 64 | bytes 512 | tf_op jit(solution)/shard_map/psum | solution.py:166
  534.7 26.1 %all-gather.9.cloned.1.call-done = f32[64,4096]{1,0:T(8,128)} async-done(((f32[64,1024]{1,0:T(8,128)}), f32[64,4096]{1,0:T(8,128)}) %all-gather.9.cloned.1.call-update) | async-done | bytes 1048592 | tf_op jit(solution)/shard_map/all_gather | solution.py:81
  562.2 29.9 %all-gather.11.cloned.1.call-done = f32[64,8192]{1,0:T(8,128)} async-done(((f32[64,1024]{1,0:T(8,128)}), f32[64,8192]{1,0:T(8,128)}) %all-gather.11.cloned.1.call-update) | async-done | bytes 2097168 | tf_op jit(solution)/shard_map/all_gather | solution.py:82
  597.0 287.9 %while.31 = (s32[]{:T(128)}, f32[1,64,32,256]{3,1,2,0:T(8,128)}, f32[1,64,16,256]{3,1,2,0:T(8,128)S(1)}, s32[8,8]{1,0:T(8,128)S(1)}, f32[8,32,256]{2,0,1:T(8,128...) while((s32[]{:T(128)}, f32[1,64,32,256]{3,1,2,0:T(8,128)}, ...), condition=%wide.region_14.19_spmd, body=%wide.region_11.18_spmd.sunk | while | flops 845842560 | bytes 8662161 | solution.py:73
  610.9 8.0 convolution_bitcast_fusion.5
  621.8 8.4 convolution_bitcast_fusion.4
  646.9 8.0 convolution_bitcast_fusion.5
  657.8 8.4 convolution_bitcast_fusion.4
  682.8 8.0 convolution_bitcast_fusion.5
  693.7 8.4 convolution_bitcast_fusion.4
  718.8 8.0 convolution_bitcast_fusion.5
  729.7 8.4 convolution_bitcast_fusion.4
  754.8 8.0 convolution_bitcast_fusion.5
  765.7 8.4 convolution_bitcast_fusion.4
  790.8 8.0 convolution_bitcast_fusion.5
  801.7 8.4 convolution_bitcast_fusion.4
  826.8 8.0 convolution_bitcast_fusion.5
  837.7 8.4 convolution_bitcast_fusion.4
  862.8 8.0 convolution_bitcast_fusion.5
  873.7 8.4 convolution_bitcast_fusion.4
  895.2 18.1 %reduce-scatter.11.cloned.1.call-done = f32[64,1024]{1,0:T(8,128)} async-done(((f32[64,4096]{1,0:T(8,128)}), f32[64,1024]{1,0:T(8,128)}) %reduce-scatter.11.cloned.1.call-update) | async-done | bytes 262160 | tf_op jit(solution)/shard_map/reduce_scatter | solution.py:88
  913.3 38.3 %reduce-scatter.9.cloned.1.call-done = f32[64,1024]{1,0:T(8,128)} async-done(((f32[64,8192]{1,0:T(8,128)}), f32[64,1024]{1,0:T(8,128)}) %reduce-scatter.9.cloned.1.call-update) | async-done | bytes 262160 | tf_op jit(solution)/shard_map/reduce_scatter | solution.py:87
  952.9 10.2 fusion.63
  963.1 38.2 %all-reduce = (f32[17,64]{0,1:T(8,128)S(1)}, f32[64]{0:T(128)S(1)}) all-reduce(f32[17,64]{0,1:T(8,128)S(1)} %bitcast.440, f32[64]{0:T(128)S(1)} %get-tuple-element.399), channel_id=1, replica_groups=mesh['row'=4,'col'=8] {'row','col'}, use_global_device_ids=true, to_apply=%region_19.24 | all-reduce | flops 1152 | bytes 9216 | tf_op jit(solution)/shard_map/psum | solution.py:151
  1009.4 41.4 %psum.47 = f32[64]{0:T(128)S(1)} all-reduce(f32[64]{0:T(128)S(1)} %get-tuple-element.397), channel_id=1, replica_groups=mesh['row'=4,'col'=8] {'row','col'}, use_global_device_ids=true, to_apply=%region_21.26 | all-reduce | flops 64 | bytes 512 | tf_op jit(solution)/shard_map/psum | solution.py:166
  (775 shorter events, 490.0 us)
Async XLA Ops:
  7.2 350.8 %copy-start = (f32[1024]{0:T(1024)S(1)}, f32[1024]{0:T(1024)}, u32[]{:S(2)}) copy-start(f32[1024]{0:T(1024)} %param.22) | copy-start | bytes 12292
  7.2 37.7 %all-gather.7.cloned.1.call-start = ((), (), s32[]{:S(2)}) async-start(), calls=%async_computation.5 | async-start | bytes 1474560 | tf_op jit(solution)/shard_map/all_gather | solution.py:81
  8.0 36.9 %copy-start.21 = (s32[1024]{0:T(1024)}, s32[1024]{0:T(1024)S(1)}, u32[]{:S(2)}) copy-start(s32[1024]{0:T(1024)S(1)} %broadcast_clamp_fusion) | copy-start | bytes 12292
  14.3 63.8 %all-gather.5.cloned.1.call-start = ((), (), s32[]{:S(2)}) async-start(), calls=%async_computation.4 | async-start | bytes 2654208 | tf_op jit(solution)/shard_map/all_gather | solution.py:82
  15.0 367.4 %reduce-scatter.7.cloned.1.call-start = ((), (), s32[]{:S(2)}) async-start(), calls=%async_computation.7 | async-start | bytes 2621440 | tf_op jit(solution)/shard_map/reduce_scatter | solution.py:88
  17.1 30.1 %copy-start.11 = (s32[8,8]{1,0:T(8,128)}, s32[8,8]{1,0:T(8,128)S(1)}, u32[]{:S(2)}) copy-start(s32[8,8]{1,0:T(8,128)S(1)} %reshape_squeeze.9) | copy-start | bytes 772
  347.6 87.1 %reduce-scatter.5.cloned.1.call-start = ((), (), s32[]{:S(2)}) async-start(), calls=%async_computation.6 | async-start | bytes 4718592 | tf_op jit(solution)/shard_map/reduce_scatter | solution.py:87
  357.9 78.1 %copy-start.5 = (f32[64,1024]{1,0:T(8,128)S(1)}, f32[64,1024]{1,0:T(8,128)}, u32[]{:S(2)}) copy-start(f32[64,1024]{1,0:T(8,128)} %param.25) | copy-start | bytes 786436
  357.9 202.9 %all-gather.9.cloned.1.call-start = ((), (), s32[]{:S(2)}) async-start(), calls=%async_computation.8 | async-start | bytes 1310720 | tf_op jit(solution)/shard_map/all_gather | solution.py:81
  363.1 127.2 %copy-start.14 = (f32[1,1024]{1,0:T(1,128)}, f32[1,1024]{1,0:T(1,128)S(1)}, u32[]{:S(2)}) copy-start(f32[1,1024]{1,0:T(1,128)S(1)} %and_select_fusion) | copy-start | bytes 12292
  491.2 104.1 %copy-start.2 = (f32[64,1024]{1,0:T(8,128)}, f32[64,1024]{1,0:T(8,128)S(1)}, u32[]{:S(2)}) copy-start(f32[64,1024]{1,0:T(8,128)S(1)} %get-tuple-element.402) | copy-start | bytes 786436
  533.3 62.0 %copy-start.23 = (f32[64]{0:T(128)}, f32[64]{0:T(128)S(1)}, u32[]{:S(2)}) copy-start(f32[64]{0:T(128)S(1)} %get-tuple-element.451) | copy-start | bytes 772
  534.1 58.0 %all-gather.11.cloned.1.call-start = ((), (), s32[]{:S(2)}) async-start(), calls=%async_computation.9 | async-start | bytes 2359296 | tf_op jit(solution)/shard_map/all_gather | solution.py:82
  534.7 378.6 %reduce-scatter.11.cloned.1.call-start = ((), (), s32[]{:S(2)}) async-start(), calls=%async_computation.11 | async-start | bytes 1310720 | tf_op jit(solution)/shard_map/reduce_scatter | solution.py:88
  597.7 10.4 copy-start.16
  597.7 10.4 copy-start.18
  633.6 10.4 copy-start.16
  633.6 10.4 copy-start.18
  669.6 10.4 copy-start.18
  705.6 10.4 copy-start.18
  741.6 10.4 copy-start.18
  777.5 10.4 copy-start.18
  813.6 10.4 copy-start.16
  813.6 10.4 copy-start.18
  849.6 10.4 copy-start.18
  886.0 65.6 %reduce-scatter.9.cloned.1.call-start = ((), (), s32[]{:S(2)}) async-start(), calls=%async_computation.10 | async-start | bytes 2359296 | tf_op jit(solution)/shard_map/reduce_scatter | solution.py:87
  890.2 61.5 %copy-start.3 = (f32[64,1024]{1,0:T(8,128)S(1)}, f32[64,1024]{1,0:T(8,128)}, u32[]{:S(2)}) copy-start(f32[64,1024]{1,0:T(8,128)} %copy-done.2) | copy-start | bytes 786436
  890.2 61.5 %copy-start.15 = (f32[1,1024]{1,0:T(1,128)S(1)}, f32[1,1024]{1,0:T(1,128)}, u32[]{:S(2)}) copy-start(f32[1,1024]{1,0:T(1,128)} %copy-done.14) | copy-start | bytes 12292
  890.2 61.5 %copy-start.24 = (f32[64]{0:T(128)S(1)}, f32[64]{0:T(128)}, u32[]{:S(2)}) copy-start(f32[64]{0:T(128)} %copy-done.23) | copy-start | bytes 772
  1001.3 50.3 %copy-start.25 = (f32[1,64]{1,0:T(1,128)S(1)}, f32[1,64]{1,0:T(1,128)}, u32[]{:S(2)}) copy-start(f32[1,64]{1,0:T(1,128)} %get-tuple-element.448) | copy-start | bytes 772
  1001.3 50.3 %copy-start.26 = (f32[1,64]{1,0:T(1,128)S(1)}, f32[1,64]{1,0:T(1,128)}, u32[]{:S(2)}) copy-start(f32[1,64]{1,0:T(1,128)} %get-tuple-element.450) | copy-start | bytes 772
  1001.3 50.9 %copy-start.1 = (f32[1024]{0:T(1024)S(1)}, f32[1024]{0:T(1024)}, u32[]{:S(2)}) copy-start(f32[1024]{0:T(1024)} %param.22) | copy-start | bytes 12292
  (72 other events, 264.2 us)
Sparse Core Ops, SparseCore 0:
  14.4 30.4 all-gather.6
  46.5 31.6 all-gather.4
  347.7 34.6 reduce-scatter.6
  384.7 49.9 reduce-scatter.4
  534.2 26.5 all-gather.8
  562.9 29.0 all-gather.10
  886.1 27.1 reduce-scatter.10
  915.6 35.9 reduce-scatter.8
where the time goes:
time: 1070 us; the launch traced here: 1060 us
  matrix products  248 us (23%)
  waiting for transfers between devices  243 us (23%)
  local copies, waits for them, and re-layouts  215 us (20%)
  other arithmetic  175 us (16%)
  blocking collectives  159 us (15%)
  between operations  14.6 us (1%)
    dot_general x16, matrix products, one_group(): direct = jnp.einsum('pgj,kgij->kpgi', col_side, stacked, precision=HIGHEST)  115 us
    dot_general x16, matrix products, one_group(): jnp.einsum('pgi,kgij->kpgj', row_side, stacked, precision=HIGHEST)  100 us
    reduce_scatter x2, waiting for transfers between devices, reduce_parts(): lax.psum_scatter(row_part, 'col', scatter_dimension=1, tiled=True)  90.6 us
    psum x2, blocking collectives, on_device(): lax.psum(jnp.sum(residual_vec * residual_vec, axis=1), ('row', 'col'))  83 us
    psum x2, blocking collectives, on_device(): lax.psum((jnp.einsum('hpn,pn->hp', earlier, image_vec, precision=HIGHEST)...  76.3 us
    while x400, local copies, waits for them, and re-layouts  72.1 us
    all_gather x2, waiting for transfers between devices, both_sides(): row_side = lax.all_gather(stacked, 'col', axis=1, tiled=True)  60.8 us
    all_gather x2, waiting for transfers between devices, both_sides(): col_side = lax.all_gather(stacked, 'row', axis=1, tiled=True)  53.2 us
  transfers between devices with their start and end apart: 8, of which 8 were waited for; matrix products, arithmetic and copies ran while one was open for 3% of the time, Pallas kernels for 0%

commit v1 on v0

v1 whole, which is shorter than its diff:
```python
import functools
import math

import jax
import jax.numpy as jnp
from jax import lax
from jax.experimental import pallas as pl
from jax.experimental.pallas import tpu as pltpu
from jax.sharding import PartitionSpec as P

BLOCK = 256
ITERS = 2
GROUP = 2

ROOT_THREE = math.sqrt(3.0)
SUPPORT = 3.0
EPSILON = 1e-06
HIGHEST = lax.Precision.HIGHEST
VMEM_LIMIT = 56 * 1024 * 1024


def split(x):
    high = x.astype(jnp.bfloat16)
    low = (x - high.astype(jnp.float32)).astype(jnp.bfloat16)
    return high, low


def mm(a, b):
    return jnp.dot(a, b, preferred_element_type=jnp.float32)


def load_values(col_values, row_values, col_t, row_v):
    devs, probes, width = col_values.shape
    per = width // BLOCK
    for dev in range(devs):
        for b in range(per):
            block = jnp.transpose(col_values[dev, :, b * BLOCK : (b + 1) * BLOCK])
            col_t[dev * per + b] = jnp.concatenate(split(block), axis=1)

    def one(dev, carry):
        for b in range(per):
            high, low = split(row_values[dev, :, b * BLOCK : (b + 1) * BLOCK])
            row_v[dev * per + b] = jnp.concatenate([high, low], axis=0)
        return carry

    lax.fori_loop(0, row_values.shape[0], one, 0)
    last = row_v.shape[0] - 1
    row_v[last] = jnp.zeros(row_v.shape[1:], jnp.bfloat16)


def products(tile_ref, at, row_at, col_at, mirror_at, col_t, row_v, row_out, col_out):
    direct = mm(tile_ref[at], col_t[col_at])
    direct = direct[:BLOCK] + direct[BLOCK:]
    direct = direct + pltpu.roll(direct, direct.shape[1] // 2, 1)
    lane = lax.broadcasted_iota(jnp.int32, direct.shape, 1)
    half = row_out.shape[1] // BLOCK
    pair = row_at // 2
    row_out[pair // half, pl.ds(pl.multiple_of(pair % half * BLOCK, BLOCK), BLOCK)] += jnp.where(
        lane // (direct.shape[1] // 2) == row_at % 2, direct, 0.0
    )
    left = row_v[mirror_at]
    mirrored = mm(left, tile_ref[at, :BLOCK]) + mm(left, tile_ref[at, BLOCK:])
    devs, probes, width = col_out.shape
    per = width // BLOCK
    col_out[col_at // per, :, pl.ds(pl.multiple_of(col_at % per * BLOCK, BLOCK), BLOCK)] += (
        mirrored[:probes] + mirrored[probes:]
    )


def evaluate(row_points_t, row_at, col_points, col_at, tile_ref, slope_ref, at):
    width = 32
    per = col_points.shape[2] // BLOCK
    feats = col_points.shape[1]
    cols = col_points[col_at // per, :, pl.ds(pl.multiple_of(col_at % per * BLOCK, BLOCK), BLOCK)]
    for chunk in range(BLOCK // width):
        low, top = chunk * width, (chunk + 1) * width
        rows = row_points_t[row_at, low:top, :]
        dist = None
        for f in range(feats):
            differ = rows[:, f : f + 1] - cols[f : f + 1, :]
            dist = differ * differ if dist is None else dist + differ * differ
        shifted = dist + EPSILON
        radius = shifted * lax.rsqrt(shifted)
        decaying = jnp.exp(-ROOT_THREE * radius)
        taper = jnp.maximum(1.0 - radius * (1.0 / SUPPORT), 0.0)
        common = decaying * (taper * taper * taper)
        first = 1.0 + ROOT_THREE * radius
        second = taper * (1.0 + (4.0 / SUPPORT) * radius)
        tile = common * (first * second)
        slope = (shifted * common) * (3.0 * second + (20.0 / (SUPPORT * SUPPORT)) * first)
        high, rest = split(tile)
        tile_ref[at, low:top] = high
        tile_ref[at, BLOCK + low : BLOCK + top] = rest
        high, rest = split(slope)
        slope_ref[at, low:top] = high
        slope_ref[at, BLOCK + low : BLOCK + top] = rest


def first_kernel(
    rows_ref, cols_ref, mirror_ref, col_points, row_points, col_values, row_values,
    tiles, row_k, row_d, col_k, col_d,
    row_points_t, slopes, col_t, row_v,
):
    step = pl.program_id(0)

    @pl.when(step == 0)
    def _():
        load_values(col_values, row_values, col_t, row_v)
        per = row_points.shape[2] // BLOCK

        def one(dev, carry):
            for b in range(per):
                row_points_t[dev * per + b] = jnp.transpose(row_points[dev, :, b * BLOCK : (b + 1) * BLOCK])
            return carry

        lax.fori_loop(0, row_points.shape[0], one, 0)
        for acc in (row_k, row_d, col_k, col_d):
            acc[...] = jnp.zeros_like(acc)

    group = tiles.shape[0]
    for g in range(group):
        t = step * group + g
        evaluate(row_points_t, rows_ref[t], col_points, cols_ref[t], tiles, slopes, g)
        products(tiles, g, rows_ref[t], cols_ref[t], mirror_ref[t], col_t, row_v, row_k, col_k)
        products(slopes, g, rows_ref[t], cols_ref[t], mirror_ref[t], col_t, row_v, row_d, col_d)


def later_kernel(
    rows_ref, cols_ref, mirror_ref, col_values, row_values, tiles,
    row_k, col_k, col_t, row_v,
):
    step = pl.program_id(0)

    @pl.when(step == 0)
    def _():
        load_values(col_values, row_values, col_t, row_v)
        for acc in (row_k, col_k):
            acc[...] = jnp.zeros_like(acc)

    group = tiles.shape[0]
    for g in range(group):
        t = step * group + g
        products(tiles, g, rows_ref[t], cols_ref[t], mirror_ref[t], col_t, row_v, row_k, col_k)


def whole_spec(shape):
    return pl.BlockSpec(shape, lambda *_: (0,) * len(shape))


def tile_products(lists, col_values, row_values, col_points=None, row_points=None, tiles=None):
    count = lists[0].shape[0]
    nr, probes, width = col_values.shape
    nc = row_values.shape[0]
    per = width // BLOCK
    f32, bf16 = jnp.float32, jnp.bfloat16
    row_shape = (nc, width // 2, 2 * probes)
    col_shape = (nr, probes, width)
    tile_shape = (count, 2 * BLOCK, BLOCK)
    group = math.gcd(GROUP, count) if tiles is None else math.gcd(4, count)
    tile_spec = pl.BlockSpec((group, 2 * BLOCK, BLOCK), lambda i, *_: (i, 0, 0))
    values_scratch = [
        pltpu.VMEM((nr * per, BLOCK, 2 * probes), bf16),
        pltpu.VMEM((nc * per + 1, 2 * probes, BLOCK), bf16),
    ]
    params = pltpu.CompilerParams(vmem_limit_bytes=VMEM_LIMIT, dimension_semantics=("arbitrary",))
    flops = 2 * count * 2 * BLOCK * BLOCK * 4 * probes
    if tiles is None:
        operands = (col_points, row_points, col_values, row_values)
        return pl.pallas_call(
            first_kernel,
            grid_spec=pltpu.PrefetchScalarGridSpec(
                num_scalar_prefetch=3,
                grid=(count // group,),
                in_specs=[whole_spec(x.shape) for x in operands],
                out_specs=[tile_spec] + [whole_spec(s) for s in (row_shape, row_shape, col_shape, col_shape)],
                scratch_shapes=[
                    pltpu.VMEM((nc * per, BLOCK, col_points.shape[1]), f32),
                    pltpu.VMEM((group, 2 * BLOCK, BLOCK), bf16),
                    *values_scratch,
                ],
            ),
            out_shape=[jax.ShapeDtypeStruct(tile_shape, bf16)]
            + [jax.ShapeDtypeStruct(s, f32) for s in (row_shape, row_shape, col_shape, col_shape)],
            compiler_params=params,
            cost_estimate=pl.CostEstimate(flops=2 * flops, bytes_accessed=32 << 20, transcendentals=2 * count * BLOCK * BLOCK),
            name="first_tiles",
        )(*lists, *operands)
    return pl.pallas_call(
        later_kernel,
        grid_spec=pltpu.PrefetchScalarGridSpec(
            num_scalar_prefetch=3,
            grid=(count // group,),
            in_specs=[whole_spec(col_values.shape), whole_spec(row_values.shape), tile_spec],
            out_specs=[whole_spec(s) for s in (row_shape, col_shape)],
            scratch_shapes=values_scratch,
        ),
        out_shape=[jax.ShapeDtypeStruct(s, f32) for s in (row_shape, col_shape)],
        compiler_params=params,
        cost_estimate=pl.CostEstimate(flops=flops, bytes_accessed=24 << 20, transcendentals=0),
        name="later_tiles",
    )(*lists, col_values, row_values, tiles)


def reduce_parts(row_part, col_part):
    from_rows = lax.psum_scatter(row_part, "col", scatter_dimension=0, tiled=False)
    from_cols = lax.psum_scatter(col_part, "row", scatter_dimension=0, tiled=False)
    probes, width = from_cols.shape
    pairs = from_rows.reshape(width // (2 * BLOCK), BLOCK, 2, probes)
    return from_cols + jnp.transpose(pairs, (3, 0, 2, 1)).reshape(probes, width)


def on_device(
    points, point_order, noise_var, inv_scale, basis_vectors, current, tile_rows, tile_cols
):
    feature_count = points.shape[0]
    per_device = points.shape[1]
    block_count = per_device // BLOCK
    row_count = lax.axis_size("row")
    col_count = lax.axis_size("col")
    point_total = per_device * row_count * col_count
    arrangement = point_order[0]
    scaled = jnp.take(points, arrangement, axis=1) * inv_scale[:, None]
    noise_here = jnp.take(noise_var, arrangement)
    row_blocks = tile_rows[0, 0]
    col_blocks = tile_cols[0, 0]
    global_row = lax.axis_index("row") * col_count * block_count + row_blocks
    global_col = (
        col_blocks // block_count * col_count + lax.axis_index("col")
    ) * block_count + col_blocks % block_count
    mirror_rows = jnp.where(global_row != global_col, row_blocks, col_count * block_count)
    lists = (row_blocks, col_blocks, mirror_rows)
    earlier = basis_vectors
    coefficient_rows = []
    for iteration in range(ITERS):
        if iteration == 0:
            stacked = jnp.concatenate([scaled, current], axis=0)
            col_side = lax.all_gather(stacked, "row", axis=0)
            row_side = lax.all_gather(stacked, "col", axis=0)
            tiles, row_k, row_d, col_k, col_d = tile_products(
                lists, col_side[:, feature_count:], row_side[:, feature_count:],
                col_side[:, :feature_count], row_side[:, :feature_count],
            )
            gradient_product = reduce_parts(row_d, col_d)
        else:
            col_side = lax.all_gather(current, "row", axis=0)
            row_side = lax.all_gather(current, "col", axis=0)
            row_k, col_k = tile_products(lists, col_side, row_side, tiles=tiles)
        image_vec = reduce_parts(row_k, col_k) + noise_here * current
        earlier_dots, alpha_now = lax.psum(
            (
                jnp.sum(earlier * image_vec[None], axis=2),
                jnp.sum(current * image_vec, axis=1),
            ),
            ("row", "col"),
        )
        earlier_dots = earlier_dots / point_total
        alpha_now = alpha_now / point_total
        residual_vec = (
            image_vec
            - alpha_now[:, None] * current
            - jnp.sum(earlier_dots[:, :, None] * earlier, axis=0)
        )
        residual_sq = (
            lax.psum(jnp.sum(residual_vec * residual_vec, axis=1), ("row", "col")) / point_total
        )
        beta_now = jnp.sqrt(residual_sq + EPSILON)
        coefficient_rows += [alpha_now, beta_now]
        if iteration + 1 < ITERS:
            earlier = jnp.concatenate([earlier, current[None]], axis=0)
        current = residual_vec / beta_now[:, None]
    return (current, jnp.stack(coefficient_rows), gradient_product)


def solution(mesh):
    return jax.shard_map(
        on_device,
        mesh=mesh,
        in_specs=(
            P(None, ("row", "col")),
            P(("row", "col"), None),
            P(("row", "col")),
            P(),
            P(None, None, ("row", "col")),
            P(None, ("row", "col")),
            P("row", "col", None),
            P("row", "col", None),
        ),
        out_specs=(P(None, ("row", "col")), P(), P(None, ("row", "col"))),
        check_vma=False,
    )
```

time: 1070 us -> 598 us (0.56)
  matrix products: 248 us -> 0 us
  local copies, waits for them, and re-layouts: 215 us -> 22.2 us
  other arithmetic: 175 us -> 22.2 us
  Pallas kernels: 0 us -> 93.7 us
  waiting for transfers between devices: 243 us -> 282 us
    dot_general x36 -> x0, matrix products: 248 us -> none  [the longest x16 115 us: one_group(): direct = jnp.einsum('pgj,kgij->kpgi', col_side, stacked, precision=HIGHEST)]
    pallas_call x0 -> x2, Pallas kernels: none -> 93.7 us  [the longest x1 72.6 us: tile_products(): pl.pallas_call(first_kernel, grid_spec=pltpu.PrefetchScalarGridSpec(num_s...]
    unnamed x8 -> x13, waiting for transfers between devices: 1.32 us -> 86.3 us
    gather x64 -> x0, local copies, waits for them, and re-layouts: 84.2 us -> none  [the longest x16 41 us: one_group(): jnp.take(row_values, row_pick, axis=1) * mirror_pick[None, :, None]]
    scatter-add x32 -> x0, other arithmetic: 84 us -> none  [the longest x16 48.3 us: one_group(): row_acc.at[:, :, row_pick].add(direct)]
    while x402 -> x0, local copies, waits for them, and re-layouts: 79.6 us -> none
    mul x8 -> x0, other arithmetic: 45.6 us -> none  [kernel_tiles(): kernel_tile = matern_part * weight]
    reduce_scatter x4 -> x3, waiting for transfers between devices: 128 us -> 82.4 us  [reduce_parts(): lax.psum_scatter(row_part, 'col', scatter_dimension=0, tiled=False)]
  transfers between devices with their start and end apart: 8 -> 10, of which waited for: 8 -> 10; matrix products, arithmetic and copies ran while one was open for 3% -> 3% of each run, Pallas kernels for 0% -> 4%
where the time goes in v1:
time: 598 us; the launch traced here: 596 us
  waiting for transfers between devices  282 us (47%)
  blocking collectives  161 us (27%)
  Pallas kernels  93.7 us (16%)
  local copies, waits for them, and re-layouts  22.2 us (4%)
  other arithmetic  22.2 us (4%)
  between operations  14.4 us (2%)
    unnamed x13, waiting for transfers between devices  86.3 us
    reduce_scatter x3, waiting for transfers between devices, reduce_parts(): lax.psum_scatter(row_part, 'col', scatter_dimension=0, tiled=False)  82.4 us
    psum x2, blocking collectives, on_device(): lax.psum(jnp.sum(residual_vec * residual_vec, axis=1), ('row', 'col'))  82.1 us
    psum x2, blocking collectives, on_device(): lax.psum((jnp.sum(earlier * image_vec[None], axis=2), jnp.sum(current * i...  79.1 us
    pallas_call x1, Pallas kernels, tile_products(): pl.pallas_call(first_kernel, grid_spec=pltpu.PrefetchScalarGridSpec(num_s...  72.6 us
    all_gather x1, waiting for transfers between devices, on_device(): row_side = lax.all_gather(current, 'col', axis=0)  31.2 us
    all_gather x1, waiting for transfers between devices, on_device(): row_side = lax.all_gather(stacked, 'col', axis=0)  29.4 us
    all_gather x1, waiting for transfers between devices, on_device(): col_side = lax.all_gather(stacked, 'row', axis=0)  28.6 us
  transfers between devices with their start and end apart: 10, of which 10 were waited for; matrix products, arithmetic and copies ran while one was open for 3% of the time, Pallas kernels for 4%

profile of v1, /device:TPU:0, one launch (start us, length us, event | category | flops | bytes accessed | tf_op | source)
XLA Modules:
  0.0 596.4 jit_solution(1969672518994517945)
XLA Ops:
  9.6 2.8 gather_fusion
  13.4 1.7 pad_maximum_fusion.1
  15.9 1.2 compare_select_fusion.3.mirror_ref
  17.1 28.6 %all-gather.9.cloned.1.call-done = f32[288,1024]{1,0:T(8,128)} async-done(((f32[72,1024]{1,0:T(8,128)}), f32[288,1024]{1,0:T(8,128)}) %all-gather.9.cloned.1.call-update) | async-done | bytes 1179664 | tf_op jit(solution)/shard_map/all_gather | solution.py:237
  45.7 1.6 slice.20.col_points
  47.3 2.3 slice.22.col_values
  49.6 29.4 %all-gather.11.cloned.1.call-done = f32[576,1024]{1,0:T(8,128)} async-done(((f32[72,1024]{1,0:T(8,128)}), f32[576,1024]{1,0:T(8,128)}) %all-gather.11.cloned.1.call-update) | async-done | bytes 2359312 | tf_op jit(solution)/shard_map/all_gather | solution.py:238
  79.0 1.7 slice.21.row_points
  80.7 3.2 slice.23.row_values
  83.8 72.6 %first_tiles.1 = (bf16[64,512,256]{2,1,0:T(8,128)(2,1)}, f32[8,512,128]{2,1,0:T(8,128)}, f32[8,512,128]{2,1,0:T(8,128)}, f32[4,64,1024]{2,1,0:T(8,128)}, f32[4,64,1024]{2,1,0:T(8,128)}) custom-call(s32[64]{0:T(128)} %bitcast.63, s32[64]{0:T(128)} %bitcast.65, s32[64]{0:T(128)} %compare_select_fusion.3.mirror_ref, f32[4,8,1024]{2,1,0:T(8,128)} %slice.20.col_points, ...), custom_call_target="tpu_custom_call" | custom-call | flops 8589934592 | bytes 33554432 | tf_op jit(solution)/shard_map/first_tiles/pallas_call | solution.py:169
  157.1 4.5 gather_fusion.1
  161.7 30.0 %reduce-scatter.13.cloned.1.call-done = f32[1,512,128]{2,1,0:T(8,128)} async-done(((f32[8,512,128]{2,1,0:T(8,128)}), f32[1,512,128]{2,1,0:T(8,128)}) %reduce-scatter.13.cloned.1.call-update) | async-done | bytes 262160 | tf_op jit(solution)/shard_map/reduce_scatter | solution.py:205
  191.7 1.1 copy.31
  193.4 27.4 %reduce-scatter.19.cloned.1.call-done = f32[1,64,1024]{2,1,0:T(8,128)} async-done(((f32[4,64,1024]{2,1,0:T(8,128)}), f32[1,64,1024]{2,1,0:T(8,128)}) %reduce-scatter.19.cloned.1.call-update) | async-done | bytes 262160
  220.8 1.1 multiply_reduce_fusion.7
  221.9 2.6 multiply_reduce_fusion.3
  224.5 39.5 %all-reduce.4 = (f32[16,64]{1,0:T(8,128)S(1)}, f32[64]{0:T(128)S(1)}) all-reduce(f32[16,64]{1,0:T(8,128)S(1)} %multiply_reduce_fusion.3, f32[64]{0:T(128)S(1)} %get-tuple-element.27), channel_id=1, replica_groups=mesh['row'=4,'col'=8] {'row','col'}, use_global_device_ids=true, to_apply=%region_5.6 | all-reduce | flops 1088 | bytes 8704 | tf_op jit(solution)/shard_map/psum | solution.py:249
  264.0 2.6 multiply_reduce_fusion.2
  266.8 41.0 %psum.44 = f32[64]{0:T(128)S(1)} all-reduce(f32[64]{0:T(128)S(1)} %get-tuple-element.25), channel_id=1, replica_groups=mesh['row'=4,'col'=8] {'row','col'}, use_global_device_ids=true, to_apply=%region_8.9 | all-reduce | flops 64 | bytes 512 | tf_op jit(solution)/shard_map/psum | solution.py:264
  310.8 24.5 %all-gather.13.cloned.1.call-done = f32[256,1024]{1,0:T(8,128)} async-done(((f32[64,1024]{1,0:T(8,128)}), f32[256,1024]{1,0:T(8,128)}) %all-gather.13.cloned.1.call-update) | async-done | bytes 1048592 | tf_op jit(solution)/shard_map/all_gather | solution.py:245
  335.2 31.2 %all-gather.15.cloned.1.call-done = f32[512,1024]{1,0:T(8,128)} async-done(((f32[64,1024]{1,0:T(8,128)}), f32[512,1024]{1,0:T(8,128)}) %all-gather.15.cloned.1.call-update) | async-done | bytes 2097168 | tf_op jit(solution)/shard_map/all_gather | solution.py:246
  366.5 21.1 %later_tiles.1 = (f32[8,512,128]{2,1,0:T(8,128)}, f32[4,64,1024]{2,1,0:T(8,128)}) custom-call(s32[64]{0:T(128)} %bitcast.64, s32[64]{0:T(128)} %bitcast.66, s32[64]{0:T(128)} %compare_select_fusion.3.mirror_ref, f32[4,64,1024]{2,1,0:T(8,128)} %bitcast.54, f32[8,64,1024]{2,1,0:T(8,128)} %bitcast.51, bf16[64,512,256]{2,1,0:T(8,128)(2,1)} %get-tuple-element.12.tiles), custom_call_target="tpu_custom_call" | custom-call | flops 4294967296 | bytes 25165824 | tf_op jit(solution)/shard_map/later_tiles/pallas_call | solution.py:188
  388.1 16.0 %reduce-scatter.17.cloned.1.call-done = f32[1,512,128]{2,1,0:T(8,128)} async-done(((f32[8,512,128]{2,1,0:T(8,128)}), f32[1,512,128]{2,1,0:T(8,128)}) %reduce-scatter.17.cloned.1.call-update) | async-done | bytes 262160 | tf_op jit(solution)/shard_map/reduce_scatter | solution.py:205
  405.9 27.9 %reduce-scatter.23.cloned.1.call-done = f32[1,64,1024]{2,1,0:T(8,128)} async-done(((f32[4,64,1024]{2,1,0:T(8,128)}), f32[1,64,1024]{2,1,0:T(8,128)}) %reduce-scatter.23.cloned.1.call-update) | async-done | bytes 262160
  433.7 1.7 bitcast_add_fusion
  435.4 36.4 %reduce-scatter.15.cloned.1.call-done = f32[1,512,128]{2,1,0:T(8,128)} async-done(((f32[8,512,128]{2,1,0:T(8,128)}), f32[1,512,128]{2,1,0:T(8,128)}) %reduce-scatter.15.cloned.1.call-update) | async-done | bytes 262160 | tf_op jit(solution)/shard_map/reduce_scatter | solution.py:205
  473.6 27.3 %reduce-scatter.21.cloned.1.call-done = f32[1,64,1024]{2,1,0:T(8,128)} async-done(((f32[4,64,1024]{2,1,0:T(8,128)}), f32[1,64,1024]{2,1,0:T(8,128)}) %reduce-scatter.21.cloned.1.call-update) | async-done | bytes 262160
  500.9 1.2 multiply_reduce_fusion.5
  502.1 2.7 multiply_reduce_fusion.1
  504.8 39.6 %all-reduce.3 = (f32[17,64]{1,0:T(8,128)S(1)}, f32[64]{0:T(128)S(1)}) all-reduce(f32[17,64]{1,0:T(8,128)S(1)} %multiply_reduce_fusion.1, f32[64]{0:T(128)S(1)} %get-tuple-element.23), channel_id=1, replica_groups=mesh['row'=4,'col'=8] {'row','col'}, use_global_device_ids=true, to_apply=%region_14.15 | all-reduce | flops 1152 | bytes 9216 | tf_op jit(solution)/shard_map/psum | solution.py:249
  544.3 2.6 multiply_reduce_fusion
  547.2 41.0 %psum.47 = f32[64]{0:T(128)S(1)} all-reduce(f32[64]{0:T(128)S(1)} %get-tuple-element.21), channel_id=1, replica_groups=mesh['row'=4,'col'=8] {'row','col'}, use_global_device_ids=true, to_apply=%region_17.18 | all-reduce | flops 64 | bytes 512 | tf_op jit(solution)/shard_map/psum | solution.py:264
  (55 shorter events, 14.1 us)
Async XLA Ops:
  7.2 150.0 %copy-start = (f32[1024]{0:T(1024)S(1)}, f32[1024]{0:T(1024)}, u32[]{:S(2)}) copy-start(f32[1024]{0:T(1024)} %param.10) | copy-start | bytes 12292
  7.2 38.5 %all-gather.9.cloned.1.call-start = ((), (), s32[]{:S(2)}) async-start(), calls=%async_computation.9 | async-start | bytes 1474560 | tf_op jit(solution)/shard_map/all_gather | solution.py:237
  15.1 63.9 %all-gather.11.cloned.1.call-start = ((), (), s32[]{:S(2)}) async-start(), calls=%async_computation.10 | async-start | bytes 2654208 | tf_op jit(solution)/shard_map/all_gather | solution.py:238
  15.9 175.8 %reduce-scatter.13.cloned.1.call-start = ((), (), s32[]{:S(2)}) async-start(), calls=%async_computation.6 | async-start | bytes 2359296 | tf_op jit(solution)/shard_map/reduce_scatter | solution.py:205
  156.5 5.2 copy-start.2
  156.5 64.3 %copy-start.1 = (f32[64,1024]{1,0:T(8,128)S(1)}, f32[64,1024]{1,0:T(8,128)}, u32[]{:S(2)}) copy-start(f32[64,1024]{1,0:T(8,128)} %param.13) | copy-start | bytes 786436
  156.5 64.2 %reduce-scatter.19.cloned.1.call-start = ((), (), s32[]{:S(2)}) async-start(), calls=%async_computation.13 | async-start | bytes 1310720
  157.1 178.1 %all-gather.13.cloned.1.call-start = ((), (), s32[]{:S(2)}) async-start(), calls=%async_computation.11 | async-start | bytes 1310720 | tf_op jit(solution)/shard_map/all_gather | solution.py:245
  308.6 57.8 %all-gather.15.cloned.1.call-start = ((), (), s32[]{:S(2)}) async-start(), calls=%async_computation.12 | async-start | bytes 2359296 | tf_op jit(solution)/shard_map/all_gather | solution.py:246
  309.2 95.0 %reduce-scatter.17.cloned.1.call-start = ((), (), s32[]{:S(2)}) async-start(), calls=%async_computation.8 | async-start | bytes 2359296 | tf_op jit(solution)/shard_map/reduce_scatter | solution.py:205
  310.0 123.8 %reduce-scatter.23.cloned.1.call-start = ((), (), s32[]{:S(2)}) async-start(), calls=%async_computation.15 | async-start | bytes 1310720
  310.7 161.2 %reduce-scatter.15.cloned.1.call-start = ((), (), s32[]{:S(2)}) async-start(), calls=%async_computation.7 | async-start | bytes 2359296 | tf_op jit(solution)/shard_map/reduce_scatter | solution.py:205
  387.5 113.4 %reduce-scatter.21.cloned.1.call-start = ((), (), s32[]{:S(2)}) async-start(), calls=%async_computation.14 | async-start | bytes 1310720
Sparse Core Ops, SparseCore 0:
  15.3 30.4 all-gather.8
  47.4 31.6 all-gather.10
  156.6 35.0 reduce-scatter.12
  194.4 26.2 reduce-scatter.18
  308.8 26.4 all-gather.12
  337.3 29.0 all-gather.14
  368.9 35.2 reduce-scatter.16
  407.3 26.3 reduce-scatter.22
  436.0 35.7 reduce-scatter.14
  474.6 26.2 reduce-scatter.20

commit v2 on v1

--- a/solution.py
+++ b/solution.py
@@ -97,11 +97,14 @@
 
 
 def first_kernel(
-    rows_ref, cols_ref, mirror_ref, col_points, row_points, col_values, row_values,
+    feats, rows_ref, cols_ref, mirror_ref, col_side, row_side,
     tiles, row_k, row_d, col_k, col_d,
     row_points_t, slopes, col_t, row_v,
 ):
     step = pl.program_id(0)
+    probes = col_side.shape[1] - feats
+    col_points, row_points = col_side.at[:, pl.ds(0, feats)], row_side.at[:, pl.ds(0, feats)]
+    col_values, row_values = col_side.at[:, pl.ds(feats, probes)], row_side.at[:, pl.ds(feats, probes)]
 
     @pl.when(step == 0)
     def _():
@@ -147,10 +150,11 @@
     return pl.BlockSpec(shape, lambda *_: (0,) * len(shape))
 
 
-def tile_products(lists, col_values, row_values, col_points=None, row_points=None, tiles=None):
+def tile_products(lists, col_side, row_side, feats, tiles=None):
     count = lists[0].shape[0]
-    nr, probes, width = col_values.shape
-    nc = row_values.shape[0]
+    nr, stacked, width = col_side.shape
+    probes = stacked - feats
+    nc = row_side.shape[0]
     per = width // BLOCK
     f32, bf16 = jnp.float32, jnp.bfloat16
     row_shape = (nc, width // 2, 2 * probes)
@@ -165,16 +169,16 @@
     params = pltpu.CompilerParams(vmem_limit_bytes=VMEM_LIMIT, dimension_semantics=("arbitrary",))
     flops = 2 * count * 2 * BLOCK * BLOCK * 4 * probes
     if tiles is None:
-        operands = (col_points, row_points, col_values, row_values)
+        operands = (col_side, row_side)
         return pl.pallas_call(
-            first_kernel,
+            functools.partial(first_kernel, feats),
             grid_spec=pltpu.PrefetchScalarGridSpec(
                 num_scalar_prefetch=3,
                 grid=(count // group,),
                 in_specs=[whole_spec(x.shape) for x in operands],
                 out_specs=[tile_spec] + [whole_spec(s) for s in (row_shape, row_shape, col_shape, col_shape)],
                 scratch_shapes=[
-                    pltpu.VMEM((nc * per, BLOCK, col_points.shape[1]), f32),
+                    pltpu.VMEM((nc * per, BLOCK, feats), f32),
                     pltpu.VMEM((group, 2 * BLOCK, BLOCK), bf16),
                     *values_scratch,
                 ],
@@ -190,7 +194,7 @@
         grid_spec=pltpu.PrefetchScalarGridSpec(
             num_scalar_prefetch=3,
             grid=(count // group,),
-            in_specs=[whole_spec(col_values.shape), whole_spec(row_values.shape), tile_spec],
+            in_specs=[whole_spec(col_side.shape), whole_spec(row_side.shape), tile_spec],
             out_specs=[whole_spec(s) for s in (row_shape, col_shape)],
             scratch_shapes=values_scratch,
         ),
@@ -198,7 +202,143 @@
         compiler_params=params,
         cost_estimate=pl.CostEstimate(flops=flops, bytes_accessed=24 << 20, transcendentals=0),
         name="later_tiles",
-    )(*lists, col_values, row_values, tiles)
+    )(*lists, col_side, row_side, tiles)
+
+
+MESH = pl.DeviceIdType.MESH
+
+
+def greet(devices):
+    barrier = pltpu.get_barrier_semaphore()
+    for device in devices:
+        pl.semaphore_signal(barrier, inc=1, device_id=device, device_id_type=MESH)
+    pl.semaphore_wait(barrier, len(devices))
+
+
+def gather_kernel(nr, nc, own, col_side, row_side, send_row, recv_row, send_col, recv_col, send_pair, local):
+    r, c = lax.axis_index("row"), lax.axis_index("col")
+    partner = c + 1 - 2 * lax.rem(c, 2)
+    along = [lax.rem(c + 2 * k, nc) for k in range(1, nc // 2)]
+    across = [lax.rem(r + k, nr) for k in range(1, nr)]
+    greet([(r, partner)] + [(r, to) for to in along] + [(to, c) for to in across])
+
+    def to_row(src, slot, sem, to):
+        return pltpu.make_async_remote_copy(
+            src_ref=src, dst_ref=row_side.at[slot], send_sem=sem, recv_sem=recv_row.at[slot],
+            device_id=(r, to), device_id_type=MESH,
+        )
+
+    def to_col(k, slot, to):
+        return pltpu.make_async_remote_copy(
+            src_ref=own, dst_ref=col_side.at[slot], send_sem=send_col.at[k], recv_sem=recv_col.at[slot],
+            device_id=(to, c), device_id_type=MESH,
+        )
+
+    sent = []
+    for k, to in enumerate(along):
+        sent.append(to_row(own, c, send_row.at[k], to))
+        sent[-1].start()
+    for k, to in enumerate(across):
+        sent.append(to_col(k, r, to))
+        sent[-1].start()
+    sent.append(to_row(own, c, send_pair.at[0], partner))
+    sent[-1].start()
+    here = [
+        pltpu.make_async_copy(own, row_side.at[c], local.at[0]),
+        pltpu.make_async_copy(own, col_side.at[r], local.at[1]),
+    ]
+    for copy in here:
+        copy.start()
+    for k in range(len(along)):
+        source = lax.rem(c + nc - 2 * (k + 1), nc)
+        to_row(own, source, send_row.at[k], source).wait_recv()
+        sent.append(to_row(row_side.at[source], source, send_pair.at[k + 1], partner))
+        sent[-1].start()
+    for k in range(nc // 2):
+        source = lax.rem(partner + nc - 2 * k, nc)
+        to_row(own, source, send_pair.at[k], partner).wait_recv()
+    for k in range(len(across)):
+        source = lax.rem(r + nr - (k + 1), nr)
+        to_col(k, source, source).wait_recv()
+    for copy in sent:
+        copy.wait_send()
+    for copy in here:
+        copy.wait()
+
+
+def both_sides(own, ident):
+    nr, nc = lax.axis_size("row"), lax.axis_size("col")
+    anywhere = pl.BlockSpec(memory_space=pl.ANY)
+    dma = pltpu.SemaphoreType.DMA
+    return pl.pallas_call(
+        functools.partial(gather_kernel, nr, nc),
+        out_shape=[jax.ShapeDtypeStruct((n, *own.shape), own.dtype) for n in (nr, nc)],
+        in_specs=[pl.BlockSpec(memory_space=pltpu.VMEM)],
+        out_specs=[anywhere, anywhere],
+        scratch_shapes=[
+            dma((nc // 2,)), dma((nc,)), dma((nr,)), dma((nr,)), dma((nc // 2,)), dma((2,)),
+        ],
+        compiler_params=pltpu.CompilerParams(collective_id=ident, has_side_effects=True),
+        name="gather_sides",
+    )(own)
+
+
+def total_kernel(nr, nc, own, out, first, second, send_one, recv_one, send_two, recv_two):
+    r, c = lax.axis_index("row"), lax.axis_index("col")
+    along = [lax.rem(c + k, nc) for k in range(1, nc)]
+    across = [lax.rem(r + k, nr) for k in range(1, nr)]
+    greet([(r, to) for to in along] + [(to, c) for to in across])
+
+    def copy_to(slots, slot, send, recv, device):
+        return pltpu.make_async_remote_copy(
+            src_ref=slots.at[slot], dst_ref=slots.at[slot], send_sem=send, recv_sem=recv.at[slot],
+            device_id=device, device_id_type=MESH,
+        )
+
+    first[c] = own[...]
+    sent = []
+    for k, to in enumerate(along):
+        sent.append(copy_to(first, c, send_one.at[k], recv_one, (r, to)))
+        sent[-1].start()
+    for k, to in enumerate(along):
+        copy_to(first, to, send_one.at[k], recv_one, (r, to)).wait_recv()
+    total = first[0]
+    for slot in range(1, nc):
+        total = total + first[slot]
+    second[r] = total
+    for k, to in enumerate(across):
+        sent.append(copy_to(second, r, send_two.at[k], recv_two, (to, c)))
+        sent[-1].start()
+    for k, to in enumerate(across):
+        copy_to(second, to, send_two.at[k], recv_two, (to, c)).wait_recv()
+    total = second[0]
+    for slot in range(1, nr):
+        total = total + second[slot]
+    out[...] = total
+    for copy in sent:
+        copy.wait_send()
+
+
+def sum_all(values, ident):
+    nr, nc = lax.axis_size("row"), lax.axis_size("col")
+    count, probes = values.shape
+    shape = (-(-count // 8) * 8, -(-probes // 128) * 128)
+    padded = jnp.pad(values, ((0, shape[0] - count), (0, shape[1] - probes)))
+    vmem = pl.BlockSpec(memory_space=pltpu.VMEM)
+    dma = pltpu.SemaphoreType.DMA
+    summed = pl.pallas_call(
+        functools.partial(total_kernel, nr, nc),
+        out_shape=jax.ShapeDtypeStruct(shape, jnp.float32),
+        in_specs=[vmem],
+        out_specs=vmem,
+        scratch_shapes=[
+            pltpu.VMEM((nc, *shape), jnp.float32), pltpu.VMEM((nr, *shape), jnp.float32),
+            dma((nc,)), dma((nc,)), dma((nr,)), dma((nr,)),
+        ],
+        compiler_params=pltpu.CompilerParams(collective_id=ident, has_side_effects=True),
+        name="sum_all",
+    )(padded)
+    return summed[:count, :probes]
 
 
 def reduce_parts(row_part, col_part):
@@ -234,34 +374,25 @@
     for iteration in range(ITERS):
         if iteration == 0:
             stacked = jnp.concatenate([scaled, current], axis=0)
-            col_side = lax.all_gather(stacked, "row", axis=0)
-            row_side = lax.all_gather(stacked, "col", axis=0)
-            tiles, row_k, row_d, col_k, col_d = tile_products(
-                lists, col_side[:, feature_count:], row_side[:, feature_count:],
-                col_side[:, :feature_count], row_side[:, :feature_count],
-            )
+            col_side, row_side = both_sides(stacked, 0)
+            tiles, row_k, row_d, col_k, col_d = tile_products(lists, col_side, row_side, feature_count)
             gradient_product = reduce_parts(row_d, col_d)
         else:
-            col_side = lax.all_gather(current, "row", axis=0)
-            row_side = lax.all_gather(current, "col", axis=0)
-            row_k, col_k = tile_products(lists, col_side, row_side, tiles=tiles)
+            col_side, row_side = both_sides(current, 1)
+            row_k, col_k = tile_products(lists, col_side, row_side, 0, tiles)
         image_vec = reduce_parts(row_k, col_k) + noise_here * current
-        earlier_dots, alpha_now = lax.psum(
-            (
-                jnp.sum(earlier * image_vec[None], axis=2),
-                jnp.sum(current * image_vec, axis=1),
-            ),
-            ("row", "col"),
-        )
-        earlier_dots = earlier_dots / point_total
-        alpha_now = alpha_now / point_total
+        partial = jnp.concatenate(
+            [jnp.sum(earlier * image_vec[None], axis=2), jnp.sum(current * image_vec, axis=1)[None]]
+        )
+        dots = sum_all(partial, 2 + 2 * iteration) / point_total
+        earlier_dots, alpha_now = dots[:-1], dots[-1]
         residual_vec = (
             image_vec
             - alpha_now[:, None] * current
             - jnp.sum(earlier_dots[:, :, None] * earlier, axis=0)
         )
         residual_sq = (
-            lax.psum(jnp.sum(residual_vec * residual_vec, axis=1), ("row", "col")) / point_total
+            sum_all(jnp.sum(residual_vec * residual_vec, axis=1)[None], 3 + 2 * iteration)[0] / point_total
         )
         beta_now = jnp.sqrt(residual_sq + EPSILON)
         coefficient_rows += [alpha_now, beta_now]

time: 598 us -> 378 us (0.63)
  blocking collectives: 161 us -> 0 us
  waiting for transfers between devices: 282 us -> 126 us
  Pallas kernels: 93.7 us -> 194 us
  local copies, waits for them, and re-layouts: 22.2 us -> 14.7 us
    psum x4 -> x0, blocking collectives: 161 us -> none  [the longest x2 82.1 us: on_device(): lax.psum(jnp.sum(residual_vec * residual_vec, axis=1), ('row', 'col'))]
    all_gather x4 -> x0, waiting for transfers between devices: 114 us -> none  [the longest x1 31.2 us: on_device(): row_side = lax.all_gather(current, 'col', axis=0)]
    pallas_call x1 -> x7, Pallas kernels: 72.6 us -> 173 us  [the longest x1 72.6 us: tile_products(): pl.pallas_call(functools.partial(first_kernel, feats), grid_spec=pltpu.Pr...]
    unnamed x13 -> x9, waiting for transfers between devices: 86.3 us -> 57.5 us
    reduce_scatter x3, waiting for transfers between devices: 82.4 us -> 68.9 us  [reduce_parts(): lax.psum_scatter(row_part, 'col', scatter_dimension=0, tiled=False)]
    slice x4 -> x3, local copies, waits for them, and re-layouts: 8.72 us -> 0.01 us  [on_device(): earlier_dots, alpha_now = (dots[:-1], dots[-1])]
  transfers between devices with their start and end apart: 10 -> 6, of which waited for: 10 -> 4; matrix products, arithmetic and copies ran while one was open for 3% -> 6% of each run, Pallas kernels for 4% -> 18%
where the time goes in v2:
time: 378 us; the launch traced here: 377 us
  Pallas kernels  194 us (51%)
  waiting for transfers between devices  126 us (33%)
  other arithmetic  27.5 us (7%)
  local copies, waits for them, and re-layouts  14.7 us (4%)
  between operations  14.4 us (4%)
    pallas_call x1, Pallas kernels, tile_products(): pl.pallas_call(functools.partial(first_kernel, feats), grid_spec=pltpu.Pr...  72.6 us
    reduce_scatter x3, waiting for transfers between devices, reduce_parts(): lax.psum_scatter(row_part, 'col', scatter_dimension=0, tiled=False)  68.9 us
    unnamed x9, waiting for transfers between devices  57.5 us
    pallas_call x2, Pallas kernels, both_sides(): pl.pallas_call(functools.partial(gather_kernel, nr, nc), out_shape=[jax.S...  54.8 us
    pallas_call x4, Pallas kernels, sum_all(): pl.pallas_call(functools.partial(total_kernel, nr, nc), out_shape=jax.Sha...  45.4 us
    pallas_call x1, Pallas kernels, tile_products(): pl.pallas_call(later_kernel, grid_spec=pltpu.PrefetchScalarGridSpec(num_s...  21.1 us
  transfers between devices with their start and end apart: 6, of which 4 were waited for; matrix products, arithmetic and copies ran while one was open for 6% of the time, Pallas kernels for 18%

profile of v2, /device:TPU:0, one launch (start us, length us, event | category | flops | bytes accessed | tf_op | source)
XLA Modules:
  0.0 376.9 jit_solution(11880754479352486392)
XLA Ops:
  8.6 1.0 copy.31
  9.6 2.8 gather_fusion
  12.6 0.7 multiply_bitcast_fusion
  13.3 1.7 pad_maximum_fusion.1.own
  15.0 30.2 %gather_sides.2 = (f32[4,72,1024]{2,1,0:T(8,128)}, f32[8,72,1024]{2,1,0:T(8,128)}) custom-call(f32[72,1024]{1,0:T(8,128)} %pad_maximum_fusion.1.own), custom_call_target="tpu_custom_call" | custom-call | tf_op jit(solution)/shard_map/gather_sides/pallas_call | solution.py:273
  45.3 1.2 compare_select_fusion.3.mirror_ref
  46.5 72.6 %first_tiles.1 = (bf16[64,512,256]{2,1,0:T(8,128)(2,1)}, f32[8,512,128]{2,1,0:T(8,128)}, f32[8,512,128]{2,1,0:T(8,128)}, f32[4,64,1024]{2,1,0:T(8,128)}, f32[4,64,1024]{2,1,0:T(8,128)}) custom-call(s32[64]{0:T(128)} %bitcast.61, s32[64]{0:T(128)} %bitcast.63, s32[64]{0:T(128)} %compare_select_fusion.3.mirror_ref, f32[4,72,1024]{2,1,0:T(8,128)} %get-tuple-element.14.col_side, ...), custom_call_target="tpu_custom_call" | custom-call | flops 8589934592 | bytes 33554432 | tf_op jit(solution)/shard_map/first_tiles/pallas_call | solution.py:173
  121.2 4.5 %gather_fusion.1 = f32[1024]{0:T(1024)S(1)} fusion(f32[1024]{0:T(1024)S(1)} %copy-done, s32[1024]{0:T(1024)S(1)} %broadcast_clamp_fusion), kind=kCustom, calls=%fused_computation.1 | custom fusion | bytes 12288 | tf_op jit(solution)/shard_map/jit(_take)/gather | solution.py:363
  125.7 33.6 %reduce-scatter.13.cloned.1.call-done = f32[1,512,128]{2,1,0:T(8,128)} async-done(((f32[8,512,128]{2,1,0:T(8,128)}), f32[1,512,128]{2,1,0:T(8,128)}) %reduce-scatter.13.cloned.1.call-update) | async-done | bytes 262160 | tf_op jit(solution)/shard_map/reduce_scatter | solution.py:345
  159.4 1.1 copy.33
  161.1 27.6 %reduce-scatter.19.cloned.1.call-done = f32[1,64,1024]{2,1,0:T(8,128)} async-done(((f32[4,64,1024]{2,1,0:T(8,128)}), f32[1,64,1024]{2,1,0:T(8,128)}) %reduce-scatter.19.cloned.1.call-update) | async-done | bytes 262160
  188.6 1.1 multiply_reduce_fusion.7
  189.7 2.6 multiply_reduce_fusion.3
  193.0 11.4 %sum_all.4 = f32[24,128]{1,0:T(8,128)} custom-call(f32[24,128]{1,0:T(8,128)} %select_maximum_fusion.1.own), custom_call_target="tpu_custom_call" | custom-call | tf_op jit(solution)/shard_map/sum_all/pallas_call | solution.py:329
  204.3 0.7 slice_multiply_fusion.1
  205.0 2.6 multiply_reduce_fusion.2
  208.5 12.0 %sum_all.5 = f32[8,128]{1,0:T(8,128)} custom-call(f32[8,128]{1,0:T(8,128)} %pad.16.own), custom_call_target="tpu_custom_call" | custom-call | tf_op jit(solution)/shard_map/sum_all/pallas_call | solution.py:329
  221.1 0.8 broadcast_divide_fusion.1.own
  221.9 24.5 %gather_sides.3 = (f32[4,64,1024]{2,1,0:T(8,128)}, f32[8,64,1024]{2,1,0:T(8,128)}) custom-call(f32[64,1024]{1,0:T(8,128)} %broadcast_divide_fusion.1.own), custom_call_target="tpu_custom_call" | custom-call | tf_op jit(solution)/shard_map/gather_sides/pallas_call | solution.py:273
  246.5 21.1 %later_tiles.1 = (f32[8,512,128]{2,1,0:T(8,128)}, f32[4,64,1024]{2,1,0:T(8,128)}) custom-call(s32[64]{0:T(128)} %bitcast.62, s32[64]{0:T(128)} %bitcast.64, s32[64]{0:T(128)} %compare_select_fusion.3.mirror_ref, f32[4,64,1024]{2,1,0:T(8,128)} %get-tuple-element.18.col_values, f32[8,64,1024]{2,1,0:T(8,128)} %get-tuple-element.19.row_values, ...), custom_call_target="tpu_custom_call" | custom-call | flops 4294967296 | bytes 25165824 | tf_op jit(solution)/shard_map/later_tiles/pallas_call | solution.py:192
  268.2 1.1 copy.37
  270.6 1.7 bitcast_add_fusion
  272.3 35.2 %reduce-scatter.15.cloned.1.call-done = f32[1,512,128]{2,1,0:T(8,128)} async-done(((f32[8,512,128]{2,1,0:T(8,128)}), f32[1,512,128]{2,1,0:T(8,128)}) %reduce-scatter.15.cloned.1.call-update) | async-done | bytes 262160 | tf_op jit(solution)/shard_map/reduce_scatter | solution.py:345
  307.5 1.1 copy.35
  309.2 27.5 %reduce-scatter.21.cloned.1.call-done = f32[1,64,1024]{2,1,0:T(8,128)} async-done(((f32[4,64,1024]{2,1,0:T(8,128)}), f32[1,64,1024]{2,1,0:T(8,128)}) %reduce-scatter.21.cloned.1.call-update) | async-done | bytes 262160
  336.7 1.2 multiply_reduce_fusion.5
  337.9 2.7 multiply_reduce_fusion.1
  341.1 11.3 %sum_all.6 = f32[24,128]{1,0:T(8,128)} custom-call(f32[24,128]{1,0:T(8,128)} %select_maximum_fusion.own), custom_call_target="tpu_custom_call" | custom-call | tf_op jit(solution)/shard_map/sum_all/pallas_call | solution.py:329
  352.5 0.7 slice_multiply_fusion
  353.2 2.6 multiply_reduce_fusion
  356.6 10.7 %sum_all.7 = f32[8,128]{1,0:T(8,128)} custom-call(f32[8,128]{1,0:T(8,128)} %pad.18.own), custom_call_target="tpu_custom_call" | custom-call | tf_op jit(solution)/shard_map/sum_all/pallas_call | solution.py:329
  368.7 0.8 broadcast_divide_fusion
  (48 shorter events, 12.3 us)
Async XLA Ops:
  7.2 114.0 %copy-start = (f32[1024]{0:T(1024)S(1)}, f32[1024]{0:T(1024)}, u32[]{:S(2)}) copy-start(f32[1024]{0:T(1024)} %param.10) | copy-start | bytes 12292
  7.2 152.2 %reduce-scatter.13.cloned.1.call-start = ((), (), s32[]{:S(2)}) async-start(), calls=%async_computation.6 | async-start | bytes 2359296 | tf_op jit(solution)/shard_map/reduce_scatter | solution.py:345
  119.0 69.6 %reduce-scatter.19.cloned.1.call-start = ((), (), s32[]{:S(2)}) async-start(), calls=%async_computation.9 | async-start | bytes 1310720
  119.1 6.6 %copy-start.2 = (s32[1,1024]{1,0:T(1,128)S(1)}, s32[1,1024]{1,0:T(1,128)}, u32[]{:S(2)}) copy-start(s32[1,1024]{1,0:T(1,128)} %param.9) | copy-start | bytes 12292
  119.8 148.4 %reduce-scatter.17.cloned.1.call-start = ((), (), s32[]{:S(2)}) async-start(), calls=%async_computation.8 | async-start | bytes 2359296 | tf_op jit(solution)/shard_map/reduce_scatter | solution.py:345
  120.5 68.1 %copy-start.1 = (f32[64,1024]{1,0:T(8,128)S(1)}, f32[64,1024]{1,0:T(8,128)}, u32[]{:S(2)}) copy-start(f32[64,1024]{1,0:T(8,128)} %param.13) | copy-start | bytes 786436
  120.5 150.1 %reduce-scatter.23.cloned.1.call-start = ((), (), s32[]{:S(2)}) async-start(), calls=%async_computation.11 | async-start | bytes 1310720
  121.1 186.4 %reduce-scatter.15.cloned.1.call-start = ((), (), s32[]{:S(2)}) async-start(), calls=%async_computation.7 | async-start | bytes 2359296 | tf_op jit(solution)/shard_map/reduce_scatter | solution.py:345
  267.6 69.1 %reduce-scatter.21.cloned.1.call-start = ((), (), s32[]{:S(2)}) async-start(), calls=%async_computation.10 | async-start | bytes 1310720
Sparse Core Ops, SparseCore 0:
  119.2 40.1 reduce-scatter.12
  162.3 26.3 reduce-scatter.18
  191.0 35.9 reduce-scatter.16
  230.0 26.8 reduce-scatter.22
  267.7 39.7 reduce-scatter.14
  310.3 26.3 reduce-scatter.20
